TPU v7x, 32 devices: a whole 2x2x4 slice. The times are simulated.
32 devices in a mesh: ctx: 8 (over z, x), head: 4 (over y, core).
Axes of the slice: x: 2, y: 2, z: 4, core: 2. Of those that a mesh axis runs over, the one named last changes fastest.
Arguments:
- activations: bfloat16 [1024, 8192], P('ctx', 'head'), may hold values from -6 to 6
- adapter_down: bfloat16 [8192, 768], P('head'), may hold values from -0.0625 to 0.0625
- adapter_ids: int32 [1024, 2], P('ctx'), may hold values from 0 to 7, all different within a row
- adapter_weight: float32 [1024, 2], P('ctx'), may hold values from 0.05 to 0.95, as said below
- query_base: bfloat16 [1024, 8192], P('ctx', 'head'), may hold values from -110 to 110
- key_base: bfloat16 [1024, 1024], P('ctx', 'head'), may hold values from -6 to 6
- value_base: bfloat16 [1024, 1024], P('ctx', 'head'), may hold values from -6 to 6
- up_query: bfloat16 [256, 8192], P(None, 'head'), may hold values from -1 to 1
- up_key: bfloat16 [256, 1024], P(None, 'head'), may hold values from -1 to 1
- up_value: bfloat16 [256, 1024], P(None, 'head'), may hold values from -1 to 1
Outputs:
- attended: bfloat16 [1024, 8192], P('ctx', 'head')
Inputs may be any that keep to these rules, and one draw needn't show every extreme that they name: `adapter_weight`: each row holds two weights that sum to one, the first the larger.
All inputs are finite; a program needn't handle non-finite values.
Results may differ from a plain program's by a relative error of at most 0.029.
Values may be sent and summed in bfloat16 or wider, within the bound.
A program may use at most 64 MiB of HBM per device.

v0:
```python
import math

import jax
import jax.numpy as jnp
from jax import lax
from jax.sharding import PartitionSpec as P

HD = 128
ADAPTERS = 8
RANK = 32


rope_base = 500000.0
floor_value = -1e30


def rotate(values, positions):
    row_count = values.shape[0]
    heads = values.shape[1] // HD
    half_width = HD // 2
    inverse = jnp.exp(jnp.arange(half_width, dtype=jnp.float32) * (-2.0 * math.log(rope_base) / HD))
    angles = positions.astype(jnp.float32)[:, None] * inverse[None, :]
    cosine = jnp.cos(angles)[:, None, :]
    sine = jnp.sin(angles)[:, None, :]
    shaped = values.reshape(row_count, heads, HD)
    first_half = shaped[:, :, :half_width]
    second_half = shaped[:, :, half_width:]
    turned = jnp.concatenate(
        [first_half * cosine - second_half * sine, second_half * cosine + first_half * sine], axis=2
    )
    return turned.reshape(row_count, heads * HD)


def mixture(adapter_ids, adapter_weight):
    labels = jnp.arange(ADAPTERS, dtype=jnp.int32)
    matches = (adapter_ids[:, :, None] == labels[None, None, :]).astype(jnp.float32)
    return jnp.sum(matches * adapter_weight[:, :, None], axis=1)


def gate_rows(low_rank, coefficient):
    row_count = low_rank.shape[0]
    shaped = low_rank.reshape(row_count, 3, ADAPTERS, RANK)
    gated = shaped * coefficient[:, None, :, None]
    return gated.astype(jnp.bfloat16).reshape(row_count, 3 * ADAPTERS * RANK)


def project(gated, query_base, key_base, value_base, up_query, up_key, up_value, positions):
    span = ADAPTERS * RANK
    query_raw = query_base.astype(jnp.float32) + jnp.dot(
        gated[:, :span], up_query, preferred_element_type=jnp.float32
    )
    key_raw = key_base.astype(jnp.float32) + jnp.dot(
        gated[:, span : 2 * span], up_key, preferred_element_type=jnp.float32
    )
    value_raw = value_base.astype(jnp.float32) + jnp.dot(
        gated[:, 2 * span :], up_value, preferred_element_type=jnp.float32
    )
    query = rotate(query_raw, positions).astype(jnp.bfloat16)
    keys = rotate(key_raw, positions).astype(jnp.bfloat16)
    return (query, keys, value_raw.astype(jnp.bfloat16))


def arrange(rows, local_kv, group_size):
    row_count = rows.shape[0]
    shaped = rows.reshape(row_count, local_kv, group_size, HD).transpose(1, 2, 0, 3)
    return shaped.reshape(local_kv, group_size * row_count, HD)


def restore(partial_value, local_kv, group_size, row_count):
    top_score, total, accum = partial_value
    normed = accum / total[:, :, None]
    shaped = normed.reshape(local_kv, group_size, row_count, HD).transpose(2, 0, 1, 3)
    return shaped.reshape(row_count, local_kv * group_size * HD).astype(jnp.bfloat16)


def on_device(
    activations,
    adapter_down,
    adapter_ids,
    adapter_weight,
    query_base,
    key_base,
    value_base,
    up_query,
    up_key,
    up_value,
):
    row_count = activations.shape[0]
    partial_low = jnp.dot(activations, adapter_down, preferred_element_type=jnp.float32)
    coefficient = mixture(adapter_ids, adapter_weight)
    low_rank = lax.psum(partial_low, "head")
    gated = gate_rows(low_rank, coefficient)
    positions = lax.axis_index("ctx") * row_count + jnp.arange(row_count, dtype=jnp.int32)
    query, keys, values = project(
        gated, query_base, key_base, value_base, up_query, up_key, up_value, positions
    )
    local_kv = keys.shape[1] // HD
    group_size = query.shape[1] // HD // local_kv
    half_rows = row_count // 2
    scale_factor = 1.0 / math.sqrt(HD)
    early_query = query[:half_rows]
    early_pos = positions[:half_rows]
    late_query = query[half_rows:]
    late_pos = positions[half_rows:]
    groups = (
        (arrange(early_query, local_kv, group_size), jnp.tile(early_pos, group_size)),
        (arrange(late_query, local_kv, group_size), jnp.tile(late_pos, group_size)),
    )
    group_rows = group_size * half_rows
    start_state = tuple(
        (
            (
                jnp.full((local_kv, group_rows), floor_value, jnp.float32),
                jnp.zeros((local_kv, group_rows), jnp.float32),
                jnp.zeros((local_kv, group_rows, HD), jnp.float32),
            )
            for entry in groups
        )
    )
    key_piece = lax.all_gather(keys, "ctx", axis=0, tiled=True)
    value_piece = lax.all_gather(values, "ctx", axis=0, tiled=True)
    piece_rows = key_piece.shape[0]
    step_rows = math.gcd(piece_rows, 512)
    step_count = piece_rows // step_rows
    key_steps = key_piece.reshape(step_count, step_rows, local_kv, HD)
    value_steps = value_piece.reshape(step_count, step_rows, local_kv, HD)

    def one_step(running, operands):
        key_block, value_block, step_index = operands
        block_start = step_index * step_rows
        key_pos = block_start + jnp.arange(step_rows, dtype=jnp.int32)
        updated = []
        for entry, partial_value in zip(groups, running):
            query_rows, query_pos = entry

            def compute(previous, query_rows=query_rows, query_pos=query_pos):
                old_top, old_total, old_accum = previous
                scores = (
                    jnp.einsum(
                        "gqd,kgd->gqk", query_rows, key_block, preferred_element_type=jnp.float32
                    )
                    * scale_factor
                )
                allowed = (query_pos[:, None] >= key_pos[None, :])[None]
                scores = jnp.where(allowed, scores, floor_value)
                new_top = jnp.maximum(old_top, jnp.max(scores, axis=2))
                shrink = jnp.exp(old_top - new_top)
                expo = jnp.where(allowed, jnp.exp(scores - new_top[:, :, None]), 0.0)
                new_total = old_total * shrink + jnp.sum(expo, axis=2)
                summed = jnp.einsum(
                    "gqk,kgd->gqd",
                    expo.astype(jnp.bfloat16),
                    value_block,
                    preferred_element_type=jnp.float32,
                )
                return (new_top, new_total, old_accum * shrink[:, :, None] + summed)

            def unchanged(previous):
                return previous

            updated.append(
                lax.cond(block_start <= jnp.max(query_pos), compute, unchanged, partial_value)
            )
        return (tuple(updated), None)

    outcome, unused = lax.scan(
        one_step, start_state, (key_steps, value_steps, jnp.arange(step_count, dtype=jnp.int32))
    )
    early_out = restore(outcome[0], local_kv, group_size, half_rows)
    late_out = restore(outcome[1], local_kv, group_size, half_rows)
    return jnp.concatenate([early_out, late_out], axis=0)


def solution(mesh):
    in_specs = (
        P("ctx", "head"),
        P("head", None),
        P("ctx", None),
        P("ctx", None),
        P("ctx", "head"),
        P("ctx", "head"),
        P("ctx", "head"),
        P(None, "head"),
        P(None, "head"),
        P(None, "head"),
    )
    out_specs = P("ctx", "head")
    return jax.shard_map(
        on_device, mesh=mesh, in_specs=in_specs, out_specs=out_specs, check_vma=False
    )
```

profile of v0, /device:TPU:26, one launch (start us, length us, event | category | flops | bytes accessed | tf_op | source)
XLA Modules:
  0.0 164.6 jit_solution(8118902472633398613)
XLA Ops:
  6.5 1.9 %copy-done = bf16[2048,768]{1,0:T(8,128)(2,1)S(1)} copy-done((bf16[2048,768]{1,0:T(8,128)(2,1)S(1)}, bf16[2048,768]{1,0:T(8,128)(2,1)}, u32[]{:S(2)}) %copy-start) | copy-done | bytes 3145752
  8.4 2.4 %fusion.36 = f32[128,768]{1,0:T(8,128)} fusion(bf16[128,2048]{1,0:T(8,128)(2,1)} %param.16, bf16[2048,768]{1,0:T(8,128)(2,1)S(1)} %copy-done), kind=kOutput, calls=%fused_computation.75 | convolution fusion | flops 402653184 | bytes 4063232 | tf_op jit(solution)/shard_map/dot_general | solution.py:89
  12.3 0.9 copy.33
  13.3 0.9 multiply_cosine_fusion
  14.2 30.3 %all-reduce.2.cloned.1.call-done = f32[128,768]{1,0:T(8,128)} async-done(((f32[128,768]{1,0:T(8,128)}), f32[128,768]{1,0:T(8,128)}) %all-reduce.2.cloned.1.call-update) | async-done | bytes 393232 | tf_op jit(solution)/shard_map/psum | solution.py:91
  44.5 1.2 multiply_convert_fusion
  45.7 1.7 %convolution_add_fusion.4 = f32[128,256]{1,0:T(8,128)} fusion(bf16[256,256]{1,0:T(8,128)(2,1)} %param.24, bf16[128,256]{1,0:T(8,128)(2,1)} %param.21, bf16[128,768]{1,0:T(8,128)(2,1)S(1)} %multiply_convert_fusion), kind=kOutput, calls=%fused_computation.42 | convolution fusion | flops 16842752 | bytes 393216 | tf_op jit(solution)/shard_map/dot_general | solution.py:52
  47.4 1.0 reshape.173
  48.4 1.1 subtract_convert_fusion.1
  49.7 33.5 %all_gather.6 = bf16[1024,256]{1,0:T(8,128)(2,1)} all-gather(bf16[128,256]{1,0:T(8,128)(2,1)S(1)} %bitcast.71), channel_id=1, replica_groups=mesh['ctx'=8,'head'=4] {'ctx'}, dimensions={0}, use_global_device_ids=true | all-gather | bytes 589824 | tf_op jit(solution)/shard_map/all_gather | solution.py:120
  83.2 2.0 %reshape.174 = bf16[2,512,2,128]{3,2,1,0:T(2,128)(2,1)} reshape(bf16[1024,256]{1,0:T(8,128)(2,1)} %all_gather.6) | data formatting | bytes 1048576 | tf_op jit(solution)/shard_map/reshape | solution.py:125
  85.2 1.1 fusion.27
  86.2 33.4 %all_gather.7 = bf16[1024,256]{1,0:T(8,128)(2,1)} all-gather(bf16[128,256]{1,0:T(8,128)(2,1)S(1)} %fusion.27), channel_id=1, replica_groups=mesh['ctx'=8,'head'=4] {'ctx'}, dimensions={0}, use_global_device_ids=true | all-gather | bytes 589824 | tf_op jit(solution)/shard_map/all_gather | solution.py:121
  119.6 2.0 %reshape.175 = bf16[2,512,2,128]{3,2,1,0:T(2,128)(2,1)} reshape(bf16[1024,256]{1,0:T(8,128)(2,1)} %all_gather.7) | data formatting | bytes 1048576 | tf_op jit(solution)/shard_map/reshape | solution.py:126
  121.6 1.7 %fusion.26 = f32[16,8,16,128]{3,1,2,0:T(8,128)S(1)} fusion(bf16[256,2048]{1,0:T(8,128)(2,1)} %param.23, bf16[128,2048]{1,0:T(8,128)(2,1)} %param.20, bf16[128,768]{1,0:T(8,128)(2,1)S(1)} %multiply_convert_fusion), kind=kOutput, calls=%fused_computation.40 | convolution fusion | flops 134742016 | bytes 2686976 | tf_op jit(solution)/shard_map/dot_general | solution.py:49
  125.9 0.8 broadcast.109.clone
  127.6 27.3 %while.23 = (s32[]{:T(128)}, f32[2,512]{1,0:T(2,128)S(1)}, f32[2,512]{1,0:T(2,128)S(1)}, f32[2,512,128]{2,1,0:T(8,128)}, f32[2,512]{1,0:T(2,128)S(1)}, /*index=5...) while((s32[]{:T(128)}, f32[2,512]{1,0:T(2,128)S(1)}, ...), condition=%wide.region_13.14_spmd.clone, body=%wide.region_4.13_spmd.clone.sunk | while | flops 551555584 | bytes 31087744 | solution.py:166
  130.2 1.4 constant_dynamic-slice_fusion.3
  132.4 4.4 %conditional.6 = ((f32[2,512]{1,0:T(2,128)S(1)}, f32[2,512]{1,0:T(2,128)S(1)}, f32[2,512,128]{2,1,0:T(8,128)})) conditional(s32[]{:T(128)} %convert_element_type.102, (f32[2,512]{1,0:T(2,128)S(1)}, f32[2,512]{1,0:T(2,128)S(1)}, f32[2,512,128]{2,1,0:T(8,128)}) %tuple.66, (s32[64]{0:T(128)S(1)}, s32[512]{0:T(512)S(1)}, bf16[2,512,128]{2,1,0:T(8,128)(2,1)}, ...), branch_computations={%region_5.5_spmd, %region_6.0_spmd} | conditional | flops 275777536 | bytes 14494068 | solution.py:162
  132.7 1.6 fusion.4
  134.9 1.1 convolution_add_fusion
  136.8 4.4 %conditional.7 = ((f32[2,512]{1,0:T(2,128)S(1)}, f32[2,512]{1,0:T(2,128)S(1)}, f32[2,512,128]{2,1,0:T(8,128)})) conditional(s32[]{:T(128)} %convert_element_type.103, (f32[2,512]{1,0:T(2,128)S(1)}, f32[2,512]{1,0:T(2,128)S(1)}, f32[2,512,128]{2,1,0:T(8,128)}) %tuple.68, (s32[64]{0:T(128)S(1)}, s32[512]{0:T(512)S(1)}, ...), branch_computations={%region_9.9_spmd, %region_10.12_spmd} | conditional | flops 275777536 | bytes 14494068 | solution.py:162
  137.1 1.6 fusion.15
  139.3 1.1 convolution_add_fusion.1
  143.9 1.4 constant_dynamic-slice_fusion.3
  146.0 4.4 %conditional.6 = ((f32[2,512]{1,0:T(2,128)S(1)}, f32[2,512]{1,0:T(2,128)S(1)}, f32[2,512,128]{2,1,0:T(8,128)})) conditional(s32[]{:T(128)} %convert_element_type.102, (f32[2,512]{1,0:T(2,128)S(1)}, f32[2,512]{1,0:T(2,128)S(1)}, f32[2,512,128]{2,1,0:T(8,128)}) %tuple.66, (s32[64]{0:T(128)S(1)}, s32[512]{0:T(512)S(1)}, bf16[2,512,128]{2,1,0:T(8,128)(2,1)}, ...), branch_computations={%region_5.5_spmd, %region_6.0_spmd} | conditional | flops 275777536 | bytes 14494068 | solution.py:162
  146.4 1.6 fusion.4
  148.6 1.1 convolution_add_fusion
  150.5 4.4 %conditional.7 = ((f32[2,512]{1,0:T(2,128)S(1)}, f32[2,512]{1,0:T(2,128)S(1)}, f32[2,512,128]{2,1,0:T(8,128)})) conditional(s32[]{:T(128)} %convert_element_type.103, (f32[2,512]{1,0:T(2,128)S(1)}, f32[2,512]{1,0:T(2,128)S(1)}, f32[2,512,128]{2,1,0:T(8,128)}) %tuple.68, (s32[64]{0:T(128)S(1)}, s32[512]{0:T(512)S(1)}, ...), branch_computations={%region_9.9_spmd, %region_10.12_spmd} | conditional | flops 275777536 | bytes 14494068 | solution.py:162
  150.8 1.6 fusion.15
  153.0 1.1 convolution_add_fusion.1
  154.9 1.3 divide_convert_fusion
  (97 shorter events, 16.3 us)
Async XLA Ops:
  6.5 1.9 %copy-start = (bf16[2048,768]{1,0:T(8,128)(2,1)S(1)}, bf16[2048,768]{1,0:T(8,128)(2,1)}, u32[]{:S(2)}) copy-start(bf16[2048,768]{1,0:T(8,128)(2,1)} %param.17) | copy-start | bytes 9437188
  6.5 5.8 %copy-start.9 = (f32[128,2]{0,1:T(2,128)S(1)}, f32[128,2]{0,1:T(2,128)}, u32[]{:S(2)}) copy-start(f32[128,2]{0,1:T(2,128)} %param.19) | copy-start | bytes 3076
  6.5 5.8 %copy-start.10 = (s32[128,2]{0,1:T(2,128)S(1)}, s32[128,2]{0,1:T(2,128)}, u32[]{:S(2)}) copy-start(s32[128,2]{0,1:T(2,128)} %param.18) | copy-start | bytes 3076
  6.5 38.0 %all-reduce.2.cloned.1.call-start = ((), (), s32[]{:S(2)}) async-start(), calls=%async_computation | async-start | bytes 786432 | tf_op jit(solution)/shard_map/psum | solution.py:91
  121.6 1.9 %copy-start.8 = (f32[128,64]{1,0:T(8,128)S(1)}, f32[128,64]{1,0:T(8,128)}, u32[]{:S(2)}) copy-start(f32[128,64]{1,0:T(8,128)} %get-tuple-element.410) | copy-start | bytes 98308
  132.7 2.2 %copy-start.1 = (bf16[512,2,128]{2,0,1:T(8,128)(2,1)S(1)}, bf16[512,2,128]{2,0,1:T(8,128)(2,1)}, u32[]{:S(2)}) copy-start(bf16[512,2,128]{2,0,1:T(8,128)(2,1)} %get-tuple-element.228) | copy-start | bytes 786436 | tf_op jit(solution)/shard_map/while/body/eval_jaxpr/cond
  132.7 2.2 %copy-start.5 = (f32[2,512,128]{2,1,0:T(8,128)S(1)}, f32[2,512,128]{2,1,0:T(8,128)}, u32[]{:S(2)}) copy-start(f32[2,512,128]{2,1,0:T(8,128)} %get-tuple-element.227) | copy-start | bytes 1572868 | tf_op jit(solution)/shard_map/while/body/eval_jaxpr/cond
  136.0 0.8 copy-start.6
  137.1 2.2 %copy-start.2 = (bf16[512,2,128]{2,0,1:T(8,128)(2,1)S(1)}, bf16[512,2,128]{2,0,1:T(8,128)(2,1)}, u32[]{:S(2)}) copy-start(bf16[512,2,128]{2,0,1:T(8,128)(2,1)} %get-tuple-element.236) | copy-start | bytes 786436 | tf_op jit(solution)/shard_map/while/body/eval_jaxpr/cond
  137.1 2.2 %copy-start.3 = (f32[2,512,128]{2,1,0:T(8,128)S(1)}, f32[2,512,128]{2,1,0:T(8,128)}, u32[]{:S(2)}) copy-start(f32[2,512,128]{2,1,0:T(8,128)} %get-tuple-element.235) | copy-start | bytes 1572868 | tf_op jit(solution)/shard_map/while/body/eval_jaxpr/cond
  140.4 0.8 copy-start.4
  146.3 2.2 %copy-start.1 = (bf16[512,2,128]{2,0,1:T(8,128)(2,1)S(1)}, bf16[512,2,128]{2,0,1:T(8,128)(2,1)}, u32[]{:S(2)}) copy-start(bf16[512,2,128]{2,0,1:T(8,128)(2,1)} %get-tuple-element.228) | copy-start | bytes 786436 | tf_op jit(solution)/shard_map/while/body/eval_jaxpr/cond
  146.4 2.2 %copy-start.5 = (f32[2,512,128]{2,1,0:T(8,128)S(1)}, f32[2,512,128]{2,1,0:T(8,128)}, u32[]{:S(2)}) copy-start(f32[2,512,128]{2,1,0:T(8,128)} %get-tuple-element.227) | copy-start | bytes 1572868 | tf_op jit(solution)/shard_map/while/body/eval_jaxpr/cond
  149.7 0.8 copy-start.6
  150.8 2.2 %copy-start.2 = (bf16[512,2,128]{2,0,1:T(8,128)(2,1)S(1)}, bf16[512,2,128]{2,0,1:T(8,128)(2,1)}, u32[]{:S(2)}) copy-start(bf16[512,2,128]{2,0,1:T(8,128)(2,1)} %get-tuple-element.236) | copy-start | bytes 786436 | tf_op jit(solution)/shard_map/while/body/eval_jaxpr/cond
  150.8 2.2 %copy-start.3 = (f32[2,512,128]{2,1,0:T(8,128)S(1)}, f32[2,512,128]{2,1,0:T(8,128)}, u32[]{:S(2)}) copy-start(f32[2,512,128]{2,1,0:T(8,128)} %get-tuple-element.235) | copy-start | bytes 1572868 | tf_op jit(solution)/shard_map/while/body/eval_jaxpr/cond
  154.1 0.8 copy-start.4
  154.9 1.6 copy-start.7
Sparse Core Ops, SparseCore 0:
  10.9 33.5 all-reduce.1
where the time goes:
time: 165 us
  blocking collectives  66.9 us (41%)
  waiting for transfers between devices  30.4 us (18%)
  local copies, waits for them, and re-layouts  20.9 us (13%)
  matrix products  17.5 us (11%)
  between operations  13.6 us (8%)
  other arithmetic  11.1 us (7%)
  loops' own time  4.26 us (3%)
    all_gather x1, blocking collectives, on_device(): key_piece = lax.all_gather(keys, 'ctx', axis=0, tiled=True)  33.5 us
    all_gather x1, blocking collectives, on_device(): value_piece = lax.all_gather(values, 'ctx', axis=0, tiled=True)  33.4 us
    psum x1, waiting for transfers between devices, on_device(): low_rank = lax.psum(partial_low, 'head')  30.3 us
    dot_general x4, matrix products, compute(): jnp.einsum('gqd,kgd->gqk', query_rows, key_block, preferred_element_type=...  6.27 us
    dynamic_slice x8, local copies, waits for them, and re-layouts, on_device(): lax.scan(one_step, start_state, (key_steps, value_steps, jnp.arange(step_...  5.65 us
    dot_general x4, matrix products, compute(): jnp.einsum('gqk,kgd->gqd', expo.astype(jnp.bfloat16), value_block, prefer...  4.32 us
    another operation x1, loops' own time, on_device(): lax.scan(one_step, start_state, (key_steps, value_steps, jnp.arange(step_...  3.97 us
  transfers between devices with their start and end apart: 1, of which 1 were waited for; matrix products, arithmetic and copies ran while one was open for 2% of the time, Pallas kernels for 0%

commit v1 on v0

v1 whole, which is shorter than its diff:
```python
import functools
import math

import jax
import jax.numpy as jnp
import numpy as np
from jax import lax
from jax.experimental import pallas as pl
from jax.experimental.pallas import tpu as pltpu
from jax.sharding import PartitionSpec as P

HD = 128
ADAPTERS = 8
RANK = 32
SPAN = ADAPTERS * RANK
ROPE_BASE = 500000.0
MASKED = -1e30
MESH = pl.DeviceIdType.MESH
CHUNKS = 4


def roll_lanes(values, shift):
    return pltpu.roll(values, shift, 1)


def spread(values):
    values = values + roll_lanes(values, 64)
    return values + roll_lanes(values, 32)


def kernel(
    n_ctx,
    n_head,
    act_hbm,
    down_hbm,
    ids_ref,
    weight_ref,
    qbase_hbm,
    kbase_hbm,
    vbase_hbm,
    upq_hbm,
    upk_hbm,
    upv_hbm,
    inverse_ref,
    out_ref,
    act,
    down,
    qbase,
    kbase,
    vbase,
    upq,
    upk,
    upv,
    low_send,
    low_recv,
    kv,
    qs,
    top,
    total,
    accum,
    cos_tab,
    sin_tab,
    in_sems,
    low_send_sems,
    low_recv_sems,
    lane_send_sems,
    cross_send_sems,
    recv_sems,
):
    ctx = lax.axis_index("ctx")
    head = lax.axis_index("head")
    z = ctx // 2
    x = ctx % 2
    n_z = n_ctx // 2
    rows, features = act.shape
    local_kv = kbase.shape[1] // HD
    group = qbase.shape[1] // HD // local_kv
    kv_width = local_kv * HD
    other = 2 * z + 1 - x

    part = features // CHUNKS
    loads = [pltpu.make_async_copy(act_hbm, act, in_sems.at[0])]
    for i in range(CHUNKS):
        piece = pl.ds(i * part, part)
        loads.append(pltpu.make_async_copy(down_hbm.at[piece], down.at[piece], in_sems.at[1 + i]))
    rest = [
        pltpu.make_async_copy(src, dst, in_sems.at[1 + CHUNKS + i])
        for i, (src, dst) in enumerate(
            ((kbase_hbm, kbase), (vbase_hbm, vbase), (upk_hbm, upk), (upv_hbm, upv), (qbase_hbm, qbase), (upq_hbm, upq))
        )
    ]
    for load in loads + rest:
        load.start()

    barrier = pltpu.get_barrier_semaphore()
    for step in range(1, n_head):
        pl.semaphore_signal(
            barrier, inc=1, device_id={"ctx": ctx, "head": lax.rem(head + step, n_head)}, device_id_type=MESH
        )
    pl.semaphore_signal(barrier, inc=1, device_id={"ctx": other, "head": head}, device_id_type=MESH)

    @pl.when(z > 0)
    def _():
        pl.semaphore_signal(barrier, inc=1, device_id={"ctx": ctx - 2, "head": head}, device_id_type=MESH)

    @pl.when(z < n_z - 1)
    def _():
        pl.semaphore_signal(barrier, inc=1, device_id={"ctx": ctx + 2, "head": head}, device_id_type=MESH)

    loads[0].wait()
    low = None
    for i in range(CHUNKS):
        loads[1 + i].wait()
        piece = pl.ds(i * part, part)
        term = jnp.dot(act[:, piece], down[piece, :], preferred_element_type=jnp.float32)
        low = term if low is None else low + term

    lane = lax.broadcasted_iota(jnp.int32, (rows, HD), 1)
    group_of = lane // RANK
    masks = []
    for j in range(2):
        chosen = ids_ref[:, j : j + 1]
        masks.append((chosen == group_of, chosen == group_of + 4))
    packs = []
    for p in range(3):
        for j in range(2):
            first, second = masks[j]
            left = low[:, p * SPAN : p * SPAN + HD]
            right = low[:, p * SPAN + HD : (p + 1) * SPAN]
            packs.append(spread(jnp.where(first, left, jnp.where(second, right, 0.0))))
    half = rows // 2
    upper = jnp.where(
        group_of == 0, packs[2], jnp.where(group_of == 1, packs[3], jnp.where(group_of == 2, packs[4], packs[5]))
    )
    half_group = group_of[:half]
    lower = jnp.where(
        half_group == 0,
        packs[0][:half],
        jnp.where(half_group == 1, packs[1][:half], jnp.where(half_group == 2, packs[0][half:], packs[1][half:])),
    )
    compact = jnp.concatenate([upper, lower], axis=0)
    low_send[...] = compact.astype(jnp.bfloat16)

    neighbours = n_head + (z > 0).astype(jnp.int32) + (z < n_z - 1).astype(jnp.int32)
    pl.semaphore_wait(barrier, neighbours)

    low_copies = []
    for step in range(n_head - 1, 0, -1):
        peer = lax.rem(head + step, n_head)
        copy = pltpu.make_async_remote_copy(
            src_ref=low_send,
            dst_ref=low_recv.at[head],
            send_sem=low_send_sems.at[step],
            recv_sem=low_recv_sems.at[head],
            device_id={"ctx": ctx, "head": peer},
            device_id_type=MESH,
        )
        copy.start()
        low_copies.append(copy)

    spot = lax.broadcasted_iota(jnp.int32, (rows, HD), 0) + ctx * rows
    angles = spot.astype(jnp.float32) * inverse_ref[...]
    cos_tab[...] = jnp.cos(angles)
    sine = jnp.sin(angles)
    sin_tab[...] = jnp.where(lane < HD // 2, -sine, sine)

    for load in rest:
        load.wait()
    for step in range(1, n_head):
        peer = lax.rem(head + step, n_head)
        pltpu.make_async_copy(low_recv.at[peer], low_recv.at[peer], low_recv_sems.at[peer]).wait()
        compact = compact + low_recv[peer].astype(jnp.float32)

    upper, lower = compact[:rows], compact[rows:]
    pieces = [
        jnp.concatenate(
            [
                spread(jnp.where(half_group == j, lower, 0.0)),
                spread(jnp.where(half_group == j + 2, lower, 0.0)),
            ],
            axis=0,
        )
        for j in range(2)
    ]
    pieces += [spread(jnp.where(group_of == k, upper, 0.0)) for k in range(4)]

    def gated_of(p):
        first = weight_ref[:, 0:1] * pieces[2 * p]
        second = weight_ref[:, 1:2] * pieces[2 * p + 1]
        sides = [
            jnp.where(masks[0][side], first, jnp.where(masks[1][side], second, 0.0)) for side in range(2)
        ]
        return jnp.concatenate(sides, axis=1).astype(jnp.bfloat16)

    def rotated(values):
        return (values * cos_tab[...] + roll_lanes(values, HD // 2) * sin_tab[...]).astype(jnp.bfloat16)

    key_raw = kbase[...].astype(jnp.float32) + jnp.dot(gated_of(1), upk[...], preferred_element_type=jnp.float32)
    for g in range(local_kv):
        kv[ctx, :, g * HD : (g + 1) * HD] = rotated(key_raw[:, g * HD : (g + 1) * HD])
    value = vbase[...].astype(jnp.float32) + jnp.dot(gated_of(2), upv[...], preferred_element_type=jnp.float32)
    kv[ctx, :, kv_width:] = value.astype(jnp.bfloat16)

    def lane_copy(block):
        return pltpu.make_async_remote_copy(
            src_ref=kv.at[block],
            dst_ref=kv.at[block],
            send_sem=lane_send_sems.at[block],
            recv_sem=recv_sems.at[block],
            device_id={"ctx": lax.rem(ctx + 2, n_ctx), "head": head},
            device_id_type=MESH,
        )

    def cross_copy(block):
        return pltpu.make_async_remote_copy(
            src_ref=kv.at[block],
            dst_ref=kv.at[block],
            send_sem=cross_send_sems.at[block],
            recv_sem=recv_sems.at[block],
            device_id={"ctx": other, "head": head},
            device_id_type=MESH,
        )

    def arrived(block):
        pltpu.make_async_copy(kv.at[block], kv.at[block], recv_sems.at[block]).wait()

    @pl.when(x == 0)
    def _():
        cross_copy(ctx).start()

    @pl.when(z < n_z - 1)
    def _():
        lane_copy(ctx).start()

    gated = gated_of(0)
    for g in range(local_kv):
        for h in range(group):
            cols = pl.ds((g * group + h) * HD, HD)
            raw = qbase[:, cols].astype(jnp.float32) + jnp.dot(
                gated, upq[:, cols], preferred_element_type=jnp.float32
            )
            qs[g, h * rows : (h + 1) * rows, :] = rotated(raw)

    factor = math.log2(math.e) / math.sqrt(HD)
    strip = 2 * rows

    def attend(block, count, diagonal):
        for g in range(local_kv):
            keys = kv[pl.ds(block, count), :, g * HD : (g + 1) * HD].reshape(count * rows, HD)
            vals = kv[pl.ds(block, count), :, kv_width + g * HD : kv_width + (g + 1) * HD].reshape(count * rows, HD)
            for c in range(group * rows // strip):
                span = pl.ds(c * strip, strip)
                scores = (
                    lax.dot_general(
                        qs[g, span, :], keys, (((1,), (1,)), ((), ())), preferred_element_type=jnp.float32
                    )
                    * factor
                )
                if diagonal:
                    row = lax.broadcasted_iota(jnp.int32, (strip, rows), 0) % rows
                    col = lax.broadcasted_iota(jnp.int32, (strip, rows), 1)
                    scores = jnp.where(row >= col, scores, MASKED)
                peak = jnp.max(scores, axis=1, keepdims=True)
                if diagonal:
                    new_top = jnp.broadcast_to(peak, (strip, HD))
                else:
                    old_top = top[g, span, :]
                    new_top = jnp.maximum(old_top, peak)
                    shrink = jnp.exp2(old_top - new_top)
                top[g, span, :] = new_top
                sums = None
                expos = []
                for k in range(count):
                    expo = jnp.exp2(scores[:, k * rows : (k + 1) * rows] - new_top)
                    sums = expo if sums is None else sums + expo
                    expos.append(expo.astype(jnp.bfloat16))
                expo = expos[0] if count == 1 else jnp.concatenate(expos, axis=1)
                summed = jnp.dot(expo, vals, preferred_element_type=jnp.float32)
                if diagonal:
                    total[g, span, :] = sums
                    accum[g, span, :] = summed
                else:
                    total[g, span, :] = total[g, span, :] * shrink + sums
                    accum[g, span, :] = accum[g, span, :] * shrink + summed

    attend(ctx, 1, True)

    def pass_on(block):
        arrived(block)

        @pl.when(z < n_z - 1)
        def _():
            lane_copy(block).start()

        cross_copy(block).start()

    @pl.when(z > 0)
    def _():
        pass_on(ctx - 2)

    @pl.when(x == 1)
    def _():
        arrived(ctx - 1)
        attend(ctx - 1, 1, False)

    def pair_step(step, carry):
        @pl.when(step < z)
        def _():
            pass_on(ctx - 2 * step - 2)

        arrived(other - 2 * step)
        attend(2 * (z - step), 2, False)
        return carry

    lax.fori_loop(1, z + 1, pair_step, 0)

    for g in range(local_kv):
        for h in range(group):
            span = pl.ds(h * rows, rows)
            whole = jnp.sum(total[g, span, :], axis=1, keepdims=True)
            cols = pl.ds((g * group + h) * HD, HD)
            out_ref[:, cols] = (accum[g, span, :] / whole).astype(jnp.bfloat16)

    for copy in low_copies:
        copy.wait_send()

    @pl.when(x == 0)
    def _():
        cross_copy(ctx).wait_send()

    @pl.when(z < n_z - 1)
    def _():
        lane_copy(ctx).wait_send()

    def drain(step, carry):
        block = ctx - 2 * step
        cross_copy(block).wait_send()

        @pl.when(z < n_z - 1)
        def _():
            lane_copy(block).wait_send()

        return carry

    lax.fori_loop(1, z + 1, drain, 0)


def on_device(
    n_ctx,
    n_head,
    activations,
    adapter_down,
    adapter_ids,
    adapter_weight,
    query_base,
    key_base,
    value_base,
    up_query,
    up_key,
    up_value,
):
    rows = activations.shape[0]
    width = query_base.shape[1]
    kv_width = key_base.shape[1]
    local_kv = kv_width // HD
    stacked = rows * (width // kv_width)
    exponent = np.arange(HD // 2, dtype=np.float32) * np.float32(-2.0 * math.log(ROPE_BASE) / HD)
    inverse = np.exp(np.concatenate([exponent, exponent])).astype(np.float32)[None, :]
    bf16, f32 = jnp.bfloat16, jnp.float32
    big = (activations, adapter_down, query_base, key_base, value_base, up_query, up_key, up_value)
    anywhere = pl.BlockSpec(memory_space=pl.ANY)
    local = pl.BlockSpec(memory_space=pltpu.VMEM)
    return pl.pallas_call(
        functools.partial(kernel, n_ctx, n_head),
        out_shape=jax.ShapeDtypeStruct((rows, width), bf16),
        in_specs=[anywhere, anywhere, local, local] + [anywhere] * 6 + [local],
        out_specs=local,
        scratch_shapes=[pltpu.VMEM(array.shape, array.dtype) for array in big]
        + [
            pltpu.VMEM((rows + rows // 2, HD), bf16),
            pltpu.VMEM((n_head, rows + rows // 2, HD), bf16),
            pltpu.VMEM((n_ctx, rows, 2 * kv_width), bf16),
            pltpu.VMEM((local_kv, stacked, HD), bf16),
            pltpu.VMEM((local_kv, stacked, HD), f32),
            pltpu.VMEM((local_kv, stacked, HD), f32),
            pltpu.VMEM((local_kv, stacked, HD), f32),
            pltpu.VMEM((rows, HD), f32),
            pltpu.VMEM((rows, HD), f32),
            pltpu.SemaphoreType.DMA((7 + CHUNKS,)),
            pltpu.SemaphoreType.DMA((n_head,)),
            pltpu.SemaphoreType.DMA((n_head,)),
            pltpu.SemaphoreType.DMA((n_ctx,)),
            pltpu.SemaphoreType.DMA((n_ctx,)),
            pltpu.SemaphoreType.DMA((n_ctx,)),
        ],
        compiler_params=pltpu.CompilerParams(
            collective_id=0, has_side_effects=True, vmem_limit_bytes=48 * 1024 * 1024
        ),
        name="lora_attention",
    )(
        activations,
        adapter_down,
        adapter_ids,
        adapter_weight,
        query_base,
        key_base,
        value_base,
        up_query,
        up_key,
        up_value,
        inverse,
    )


def solution(mesh):
    in_specs = (
        P("ctx", "head"),
        P("head", None),
        P("ctx", None),
        P("ctx", None),
        P("ctx", "head"),
        P("ctx", "head"),
        P("ctx", "head"),
        P(None, "head"),
        P(None, "head"),
        P(None, "head"),
    )
    return jax.shard_map(
        functools.partial(on_device, mesh.shape["ctx"], mesh.shape["head"]),
        mesh=mesh,
        in_specs=in_specs,
        out_specs=P("ctx", "head"),
        check_vma=False,
    )
```

time: 165 us -> 34.4 us (0.21)
  the two profiles are of different devices: /device:TPU:26 before, /device:TPU:24 now
where the time goes in v1:
time: 34.4 us; the launch traced here: 34 us
  Pallas kernels  24.2 us (70%)
  local copies, waits for them, and re-layouts  9.81 us (29%)
    pallas_call x1, Pallas kernels, on_device(): pl.pallas_call(functools.partial(kernel, n_ctx, n_head), out_shape=jax.Sh...  24.2 us
    unnamed x19, local copies, waits for them, and re-layouts  9.81 us

profile of v1, /device:TPU:24, one launch (start us, length us, event | category | flops | bytes accessed | tf_op | source)
XLA Modules:
  0.0 34.0 jit_solution(15684443887888496903)
XLA Ops:
  0.0 0.8 %copy.12.ids_ref = s32[128,2]{1,0:T(8,128)S(1)} copy(s32[128,2]{0,1:T(2,128)} %param.13) | data formatting | bytes 2048 | tf_op args[2]
  0.8 0.8 %copy.13.weight_ref = f32[128,2]{1,0:T(8,128)S(1)} copy(f32[128,2]{0,1:T(2,128)} %param.14) | data formatting | bytes 2048 | tf_op args[3]
  1.6 0.0 copy-start
  1.6 1.2 %copy-done = bf16[256,2048]{1,0:T(8,128)(2,1)S(1)} copy-done((bf16[256,2048]{1,0:T(8,128)(2,1)S(1)}, bf16[256,2048]{1,0:T(8,128)(2,1)}, u32[]{:S(2)}) %copy-start) | copy-done | bytes 1048600
  2.8 0.0 copy-start.1
  2.8 1.0 %copy-done.1 = bf16[128,2048]{1,0:T(8,128)(2,1)S(1)} copy-done((bf16[128,2048]{1,0:T(8,128)(2,1)S(1)}, bf16[128,2048]{1,0:T(8,128)(2,1)}, u32[]{:S(2)}) %copy-start.1) | copy-done | bytes 524312
  3.8 0.0 copy-start.2
  3.8 1.0 %copy-done.2 = bf16[128,2048]{1,0:T(8,128)(2,1)S(1)} copy-done((bf16[128,2048]{1,0:T(8,128)(2,1)S(1)}, bf16[128,2048]{1,0:T(8,128)(2,1)}, u32[]{:S(2)}) %copy-start.2) | copy-done | bytes 524312
  4.9 0.0 copy-start.3
  4.9 0.9 %copy-done.3 = bf16[256,256]{1,0:T(8,128)(2,1)S(1)} copy-done((bf16[256,256]{1,0:T(8,128)(2,1)S(1)}, bf16[256,256]{1,0:T(8,128)(2,1)}, u32[]{:S(2)}) %copy-start.3) | copy-done | bytes 131096
  5.8 0.0 copy-start.4
  5.8 0.9 %copy-done.4 = bf16[256,256]{1,0:T(8,128)(2,1)S(1)} copy-done((bf16[256,256]{1,0:T(8,128)(2,1)S(1)}, bf16[256,256]{1,0:T(8,128)(2,1)}, u32[]{:S(2)}) %copy-start.4) | copy-done | bytes 131096
  6.7 0.0 copy-start.5
  6.7 0.8 %copy-done.5 = bf16[128,256]{1,0:T(8,128)(2,1)S(1)} copy-done((bf16[128,256]{1,0:T(8,128)(2,1)S(1)}, bf16[128,256]{1,0:T(8,128)(2,1)}, u32[]{:S(2)}) %copy-start.5) | copy-done | bytes 65560
  7.5 0.0 copy-start.6
  7.5 0.8 %copy-done.6 = bf16[128,256]{1,0:T(8,128)(2,1)S(1)} copy-done((bf16[128,256]{1,0:T(8,128)(2,1)S(1)}, bf16[128,256]{1,0:T(8,128)(2,1)}, u32[]{:S(2)}) %copy-start.6) | copy-done | bytes 65560
  8.4 0.0 copy-start.7
  8.4 0.7 %copy-done.7 = f32[1,128]{1,0:T(1,128)S(1)} copy-done((f32[1,128]{1,0:T(1,128)S(1)}, f32[1,128]{1,0:T(1,128)}, u32[]{:S(2)}) %copy-start.7) | copy-done | bytes 536
  9.0 24.2 %lora_attention.1 = bf16[128,2048]{1,0:T(8,128)(2,1)S(1)} custom-call(bf16[128,2048]{1,0:T(8,128)(2,1)S(1)} %copy-done.1, bf16[2048,768]{1,0:T(8,128)(2,1)} %down_hbm.1, s32[128,2]{1,0:T(8,128)S(1)} %copy.12.ids_ref, f32[128,2]{1,0:T(8,128)S(1)} %copy.13.weight_ref, bf16[128,2048]{1,0:T(8,128)(2,1)S(1)} %copy-done.2, bf16[128,256]{1,0:T(8,128)(2,1)S(1)} %copy-done.5, ...), custom_call_target="tpu_custom_call" | custom-call | tf_op jit(solution)/shard_map/lora_attention/pallas_call | solution.py:373
  33.2 0.8 %copy.15 = bf16[128,2048]{1,0:T(8,128)(2,1)} copy(bf16[128,2048]{1,0:T(8,128)(2,1)S(1)} %lora_attention.1) | data formatting | bytes 1048576
Async XLA Ops:
  1.6 1.2 %copy-start = (bf16[256,2048]{1,0:T(8,128)(2,1)S(1)}, bf16[256,2048]{1,0:T(8,128)(2,1)}, u32[]{:S(2)}) copy-start(bf16[256,2048]{1,0:T(8,128)(2,1)} %upq_hbm.1) | copy-start | bytes 3145732
  2.8 1.0 %copy-start.1 = (bf16[128,2048]{1,0:T(8,128)(2,1)S(1)}, bf16[128,2048]{1,0:T(8,128)(2,1)}, u32[]{:S(2)}) copy-start(bf16[128,2048]{1,0:T(8,128)(2,1)} %act_hbm.1) | copy-start | bytes 1572868
  3.8 1.0 %copy-start.2 = (bf16[128,2048]{1,0:T(8,128)(2,1)S(1)}, bf16[128,2048]{1,0:T(8,128)(2,1)}, u32[]{:S(2)}) copy-start(bf16[128,2048]{1,0:T(8,128)(2,1)} %qbase_hbm.1) | copy-start | bytes 1572868
  4.9 0.9 %copy-start.3 = (bf16[256,256]{1,0:T(8,128)(2,1)S(1)}, bf16[256,256]{1,0:T(8,128)(2,1)}, u32[]{:S(2)}) copy-start(bf16[256,256]{1,0:T(8,128)(2,1)} %upk_hbm.1) | copy-start | bytes 393220
  5.8 0.9 %copy-start.4 = (bf16[256,256]{1,0:T(8,128)(2,1)S(1)}, bf16[256,256]{1,0:T(8,128)(2,1)}, u32[]{:S(2)}) copy-start(bf16[256,256]{1,0:T(8,128)(2,1)} %upv_hbm.1) | copy-start | bytes 393220
  6.7 0.8 %copy-start.5 = (bf16[128,256]{1,0:T(8,128)(2,1)S(1)}, bf16[128,256]{1,0:T(8,128)(2,1)}, u32[]{:S(2)}) copy-start(bf16[128,256]{1,0:T(8,128)(2,1)} %kbase_hbm.1) | copy-start | bytes 196612
  7.5 0.8 %copy-start.6 = (bf16[128,256]{1,0:T(8,128)(2,1)S(1)}, bf16[128,256]{1,0:T(8,128)(2,1)}, u32[]{:S(2)}) copy-start(bf16[128,256]{1,0:T(8,128)(2,1)} %vbase_hbm.1) | copy-start | bytes 196612
  8.4 0.7 %copy-start.7 = (f32[1,128]{1,0:T(1,128)S(1)}, f32[1,128]{1,0:T(1,128)}, u32[]{:S(2)}) copy-start(f32[1,128]{1,0:T(1,128)} %constant.2.clone.inverse_ref) | copy-start | bytes 1540

commit v2 on v1

--- a/solution.py
+++ b/solution.py
@@ -28,29 +28,36 @@
     return values + roll_lanes(values, 32)
 
 
+def columns(row, rows):
+    return jnp.broadcast_to(row, (HD, rows)).T
+
+
 def kernel(
     n_ctx,
     n_head,
     act_hbm,
     down_hbm,
-    ids_ref,
-    weight_ref,
+    ids_hbm,
+    weight_hbm,
     qbase_hbm,
     kbase_hbm,
     vbase_hbm,
     upq_hbm,
     upk_hbm,
     upv_hbm,
-    inverse_ref,
+    inverse_hbm,
     out_ref,
     act,
     down,
+    ids_ref,
+    weight_ref,
     qbase,
     kbase,
     vbase,
     upq,
     upk,
     upv,
+    inverse_ref,
     low_send,
     low_recv,
     kv,
@@ -75,7 +82,6 @@
     rows, features = act.shape
     local_kv = kbase.shape[1] // HD
     group = qbase.shape[1] // HD // local_kv
-    kv_width = local_kv * HD
     other = 2 * z + 1 - x
 
     part = features // CHUNKS
@@ -86,10 +92,11 @@
     rest = [
         pltpu.make_async_copy(src, dst, in_sems.at[1 + CHUNKS + i])
         for i, (src, dst) in enumerate(
-            ((kbase_hbm, kbase), (vbase_hbm, vbase), (upk_hbm, upk), (upv_hbm, upv), (qbase_hbm, qbase), (upq_hbm, upq))
+            ((ids_hbm, ids_ref), (weight_hbm, weight_ref), (inverse_hbm, inverse_ref), (kbase_hbm, kbase), (vbase_hbm, vbase), (upk_hbm, upk), (upv_hbm, upv), (qbase_hbm, qbase), (upq_hbm, upq))
         )
     ]
-    for load in loads + rest:
+    small, rest = rest[:3], rest[3:]
+    for load in small + loads + rest:
         load.start()
 
     barrier = pltpu.get_barrier_semaphore()
@@ -115,12 +122,15 @@
         term = jnp.dot(act[:, piece], down[piece, :], preferred_element_type=jnp.float32)
         low = term if low is None else low + term
 
+    for load in small:
+        load.wait()
     lane = lax.broadcasted_iota(jnp.int32, (rows, HD), 1)
     group_of = lane // RANK
+    group_value = group_of.astype(jnp.float32)
     masks = []
     for j in range(2):
-        chosen = ids_ref[:, j : j + 1]
-        masks.append((chosen == group_of, chosen == group_of + 4))
+        chosen = columns(ids_ref[j : j + 1, :].astype(jnp.float32), rows)
+        masks.append((chosen == group_value, chosen == group_value + 4.0))
     packs = []
     for p in range(3):
         for j in range(2):
@@ -184,9 +194,11 @@
     ]
     pieces += [spread(jnp.where(group_of == k, upper, 0.0)) for k in range(4)]
 
+    shares = [columns(weight_ref[j : j + 1, :], rows) for j in range(2)]
+
     def gated_of(p):
-        first = weight_ref[:, 0:1] * pieces[2 * p]
-        second = weight_ref[:, 1:2] * pieces[2 * p + 1]
+        first = shares[0] * pieces[2 * p]
+        second = shares[1] * pieces[2 * p + 1]
         sides = [
             jnp.where(masks[0][side], first, jnp.where(masks[1][side], second, 0.0)) for side in range(2)
         ]
@@ -197,40 +209,43 @@
 
     key_raw = kbase[...].astype(jnp.float32) + jnp.dot(gated_of(1), upk[...], preferred_element_type=jnp.float32)
     for g in range(local_kv):
-        kv[ctx, :, g * HD : (g + 1) * HD] = rotated(key_raw[:, g * HD : (g + 1) * HD])
+        kv[ctx, g, :, :HD] = rotated(key_raw[:, g * HD : (g + 1) * HD])
     value = vbase[...].astype(jnp.float32) + jnp.dot(gated_of(2), upv[...], preferred_element_type=jnp.float32)
-    kv[ctx, :, kv_width:] = value.astype(jnp.bfloat16)
-
-    def lane_copy(block):
+    for g in range(local_kv):
+        kv[ctx, g, :, HD:] = value[:, g * HD : (g + 1) * HD].astype(jnp.bfloat16)
+
+    def lane_copy(block, g):
         return pltpu.make_async_remote_copy(
-            src_ref=kv.at[block],
-            dst_ref=kv.at[block],
-            send_sem=lane_send_sems.at[block],
-            recv_sem=recv_sems.at[block],
+            src_ref=kv.at[block, g],
+            dst_ref=kv.at[block, g],
+            send_sem=lane_send_sems.at[block, g],
+            recv_sem=recv_sems.at[block, g],
             device_id={"ctx": lax.rem(ctx + 2, n_ctx), "head": head},
             device_id_type=MESH,
         )
 
-    def cross_copy(block):
+    def cross_copy(block, g):
         return pltpu.make_async_remote_copy(
-            src_ref=kv.at[block],
-            dst_ref=kv.at[block],
-            send_sem=cross_send_sems.at[block],
-            recv_sem=recv_sems.at[block],
+            src_ref=kv.at[block, g],
+            dst_ref=kv.at[block, g],
+            send_sem=cross_send_sems.at[block, g],
+            recv_sem=recv_sems.at[block, g],
             device_id={"ctx": other, "head": head},
             device_id_type=MESH,
         )
 
-    def arrived(block):
-        pltpu.make_async_copy(kv.at[block], kv.at[block], recv_sems.at[block]).wait()
-
-    @pl.when(x == 0)
-    def _():
-        cross_copy(ctx).start()
-
-    @pl.when(z < n_z - 1)
-    def _():
-        lane_copy(ctx).start()
+    def arrived(block, g):
+        pltpu.make_async_copy(kv.at[block, g], kv.at[block, g], recv_sems.at[block, g]).wait()
+
+    for g in range(local_kv):
+
+        @pl.when(x == 0)
+        def _():
+            cross_copy(ctx, g).start()
+
+        @pl.when(z < n_z - 1)
+        def _():
+            lane_copy(ctx, g).start()
 
     gated = gated_of(0)
     for g in range(local_kv):
@@ -244,72 +259,76 @@
     factor = math.log2(math.e) / math.sqrt(HD)
     strip = 2 * rows
 
-    def attend(block, count, diagonal):
+    def attend(block, count, diagonal, g):
+        keys = kv[pl.ds(block, count), g, :, :HD].reshape(count * rows, HD)
+        vals = kv[pl.ds(block, count), g, :, HD:].reshape(count * rows, HD)
+        for c in range(group * rows // strip):
+            span = pl.ds(c * strip, strip)
+            scores = (
+                lax.dot_general(
+                    qs[g, span, :], keys, (((1,), (1,)), ((), ())), preferred_element_type=jnp.float32
+                )
+                * factor
+            )
+            if diagonal:
+                row = lax.broadcasted_iota(jnp.int32, (strip, rows), 0) % rows
+                col = lax.broadcasted_iota(jnp.int32, (strip, rows), 1)
+                scores = jnp.where(row >= col, scores, MASKED)
+            peak = jnp.max(scores, axis=1, keepdims=True)
+            if diagonal:
+                new_top = jnp.broadcast_to(peak, (strip, HD))
+            else:
+                old_top = top[g, span, :]
+                new_top = jnp.maximum(old_top, peak)
+                shrink = jnp.exp2(old_top - new_top)
+            top[g, span, :] = new_top
+            sums = None
+            expos = []
+            for k in range(count):
+                expo = jnp.exp2(scores[:, k * rows : (k + 1) * rows] - new_top)
+                sums = expo if sums is None else sums + expo
+                expos.append(expo.astype(jnp.bfloat16))
+            expo = expos[0] if count == 1 else jnp.concatenate(expos, axis=1)
+            summed = jnp.dot(expo, vals, preferred_element_type=jnp.float32)
+            if diagonal:
+                total[g, span, :] = sums
+                accum[g, span, :] = summed
+            else:
+                total[g, span, :] = total[g, span, :] * shrink + sums
+                accum[g, span, :] = accum[g, span, :] * shrink + summed
+
+    def pass_on(block, g):
+        arrived(block, g)
+
+        @pl.when(z < n_z - 1)
+        def _():
+            lane_copy(block, g).start()
+
+        cross_copy(block, g).start()
+
+    for g in range(local_kv):
+        attend(ctx, 1, True, g)
+
+    for g in range(local_kv):
+
+        @pl.when(z > 0)
+        def _():
+            pass_on(ctx - 2, g)
+
+        @pl.when(x == 1)
+        def _():
+            arrived(ctx - 1, g)
+            attend(ctx - 1, 1, False, g)
+
+    def pair_step(step, carry):
         for g in range(local_kv):
-            keys = kv[pl.ds(block, count), :, g * HD : (g + 1) * HD].reshape(count * rows, HD)
-            vals = kv[pl.ds(block, count), :, kv_width + g * HD : kv_width + (g + 1) * HD].reshape(count * rows, HD)
-            for c in range(group * rows // strip):
-                span = pl.ds(c * strip, strip)
-                scores = (
-                    lax.dot_general(
-                        qs[g, span, :], keys, (((1,), (1,)), ((), ())), preferred_element_type=jnp.float32
-                    )
-                    * factor
-                )
-                if diagonal:
-                    row = lax.broadcasted_iota(jnp.int32, (strip, rows), 0) % rows
-                    col = lax.broadcasted_iota(jnp.int32, (strip, rows), 1)
-                    scores = jnp.where(row >= col, scores, MASKED)
-                peak = jnp.max(scores, axis=1, keepdims=True)
-                if diagonal:
-                    new_top = jnp.broadcast_to(peak, (strip, HD))
-                else:
-                    old_top = top[g, span, :]
-                    new_top = jnp.maximum(old_top, peak)
-                    shrink = jnp.exp2(old_top - new_top)
-                top[g, span, :] = new_top
-                sums = None
-                expos = []
-                for k in range(count):
-                    expo = jnp.exp2(scores[:, k * rows : (k + 1) * rows] - new_top)
-                    sums = expo if sums is None else sums + expo
-                    expos.append(expo.astype(jnp.bfloat16))
-                expo = expos[0] if count == 1 else jnp.concatenate(expos, axis=1)
-                summed = jnp.dot(expo, vals, preferred_element_type=jnp.float32)
-                if diagonal:
-                    total[g, span, :] = sums
-                    accum[g, span, :] = summed
-                else:
-                    total[g, span, :] = total[g, span, :] * shrink + sums
-                    accum[g, span, :] = accum[g, span, :] * shrink + summed
-
-    attend(ctx, 1, True)
-
-    def pass_on(block):
-        arrived(block)
-
-        @pl.when(z < n_z - 1)
-        def _():
-            lane_copy(block).start()
-
-        cross_copy(block).start()
-
-    @pl.when(z > 0)
-    def _():
-        pass_on(ctx - 2)
-
-    @pl.when(x == 1)
-    def _():
-        arrived(ctx - 1)
-        attend(ctx - 1, 1, False)
-
-    def pair_step(step, carry):
-        @pl.when(step < z)
-        def _():
-            pass_on(ctx - 2 * step - 2)
-
-        arrived(other - 2 * step)
-        attend(2 * (z - step), 2, False)
+
+            @pl.when(step < z)
+            def _():
+                pass_on(ctx - 2 * step - 2, g)
+
+            arrived(other - 2 * step, g)
+            attend(2 * (z - step), 2, False, g)
         return carry
 
     lax.fori_loop(1, z + 1, pair_step, 0)
@@ -324,21 +343,24 @@
     for copy in low_copies:
         copy.wait_send()
 
-    @pl.when(x == 0)
-    def _():
-        cross_copy(ctx).wait_send()
-
-    @pl.when(z < n_z - 1)
-    def _():
-        lane_copy(ctx).wait_send()
+    for g in range(local_kv):
+
+        @pl.when(x == 0)
+        def _():
+            cross_copy(ctx, g).wait_send()
+
+        @pl.when(z < n_z - 1)
+        def _():
+            lane_copy(ctx, g).wait_send()
 
     def drain(step, carry):
         block = ctx - 2 * step
-        cross_copy(block).wait_send()
-
-        @pl.when(z < n_z - 1)
-        def _():
-            lane_copy(block).wait_send()
+        for g in range(local_kv):
+            cross_copy(block, g).wait_send()
+
+            @pl.when(z < n_z - 1)
+            def _():
+                lane_copy(block, g).wait_send()
 
         return carry
 
@@ -367,34 +389,35 @@
     exponent = np.arange(HD // 2, dtype=np.float32) * np.float32(-2.0 * math.log(ROPE_BASE) / HD)
     inverse = np.exp(np.concatenate([exponent, exponent])).astype(np.float32)[None, :]
     bf16, f32 = jnp.bfloat16, jnp.float32
-    big = (activations, adapter_down, query_base, key_base, value_base, up_query, up_key, up_value)
+    adapter_ids, adapter_weight = adapter_ids.T, adapter_weight.T
+    big = (activations, adapter_down, adapter_ids, adapter_weight, query_base, key_base, value_base, up_query, up_key, up_value, inverse)
     anywhere = pl.BlockSpec(memory_space=pl.ANY)
     local = pl.BlockSpec(memory_space=pltpu.VMEM)
     return pl.pallas_call(
         functools.partial(kernel, n_ctx, n_head),
         out_shape=jax.ShapeDtypeStruct((rows, width), bf16),
-        in_specs=[anywhere, anywhere, local, local] + [anywhere] * 6 + [local],
+        in_specs=[anywhere] * 11,
         out_specs=local,
         scratch_shapes=[pltpu.VMEM(array.shape, array.dtype) for array in big]
         + [
             pltpu.VMEM((rows + rows // 2, HD), bf16),
             pltpu.VMEM((n_head, rows + rows // 2, HD), bf16),
-            pltpu.VMEM((n_ctx, rows, 2 * kv_width), bf16),
+            pltpu.VMEM((n_ctx, local_kv, rows, 2 * HD), bf16),
             pltpu.VMEM((local_kv, stacked, HD), bf16),
             pltpu.VMEM((local_kv, stacked, HD), f32),
             pltpu.VMEM((local_kv, stacked, HD), f32),
             pltpu.VMEM((local_kv, stacked, HD), f32),
             pltpu.VMEM((rows, HD), f32),
             pltpu.VMEM((rows, HD), f32),
-            pltpu.SemaphoreType.DMA((7 + CHUNKS,)),
+            pltpu.SemaphoreType.DMA((10 + CHUNKS,)),
             pltpu.SemaphoreType.DMA((n_head,)),
             pltpu.SemaphoreType.DMA((n_head,)),
-            pltpu.SemaphoreType.DMA((n_ctx,)),
-            pltpu.SemaphoreType.DMA((n_ctx,)),
-            pltpu.SemaphoreType.DMA((n_ctx,)),
+            pltpu.SemaphoreType.DMA((n_ctx, local_kv)),
+            pltpu.SemaphoreType.DMA((n_ctx, local_kv)),
+            pltpu.SemaphoreType.DMA((n_ctx, local_kv)),
         ],
         compiler_params=pltpu.CompilerParams(
-            collective_id=0, has_side_effects=True, vmem_limit_bytes=48 * 1024 * 1024
+            collective_id=0, has_side_effects=True, vmem_limit_bytes=63 * 1024 * 1024
         ),
         name="lora_attention",
     )(

time: 34.4 us -> 26.1 us (0.76)
  local copies, waits for them, and re-layouts: 9.81 us -> 1.88 us
    unnamed x19 -> x1, local copies, waits for them, and re-layouts: 9.81 us -> 1.88 us
where the time goes in v2:
time: 26.1 us; the launch traced here: 25.9 us
  Pallas kernels  24 us (92%)
  local copies, waits for them, and re-layouts  1.88 us (7%)
    pallas_call x1, Pallas kernels, on_device(): pl.pallas_call(functools.partial(kernel, n_ctx, n_head), out_shape=jax.Sh...  24 us
    unnamed x1, local copies, waits for them, and re-layouts  1.88 us

profile of v2, /device:TPU:24, one launch (start us, length us, event | category | flops | bytes accessed | tf_op | source)
XLA Modules:
  0.0 25.9 jit_solution(9539800654572846801)
XLA Ops:
  0.0 24.0 %lora_attention.1 = bf16[128,2048]{1,0:T(8,128)(2,1)} custom-call(bf16[128,2048]{1,0:T(8,128)(2,1)} %act_hbm.1, bf16[2048,768]{1,0:T(8,128)(2,1)} %down_hbm.1, s32[2,128]{1,0:T(2,128)} %bitcast.2, f32[2,128]{1,0:T(2,128)} %bitcast.3, bf16[128,2048]{1,0:T(8,128)(2,1)} %qbase_hbm.1, bf16[128,256]{1,0:T(8,128)(2,1)} %kbase_hbm.1, bf16[128,256]{1,0:T(8,128)(2,1)} %vbase_hbm.1, ...), custom_call_target="tpu_custom_call" | custom-call | tf_op jit(solution)/shard_map/lora_attention/pallas_call | solution.py:396
  24.0 1.9 %copy.13 = bf16[128,2048]{1,0:T(8,128)(2,1)} copy(bf16[128,2048]{1,0:T(8,128)(2,1)} %lora_attention.1) | data formatting | bytes 1048576

commit v3 on v2

--- a/solution.py
+++ b/solution.py
@@ -234,12 +234,17 @@
             device_id_type=MESH,
         )
 
+    last = local_kv - 1
+
+    def crosses_own(g):
+        return jnp.logical_or(x == 0, z == 0) if g == last else x == 0
+
     def arrived(block, g):
         pltpu.make_async_copy(kv.at[block, g], kv.at[block, g], recv_sems.at[block, g]).wait()
 
     for g in range(local_kv):
 
-        @pl.when(x == 0)
+        @pl.when(crosses_own(g))
         def _():
             cross_copy(ctx, g).start()
 
@@ -297,14 +302,27 @@
                 total[g, span, :] = total[g, span, :] * shrink + sums
                 accum[g, span, :] = accum[g, span, :] * shrink + summed
 
-    def pass_on(block, g):
+    def send_on(block, g):
+        @pl.when(z < n_z - 1)
+        def _():
+            lane_copy(block, g).start()
+
+    def pass_on(block, g, is_first):
         arrived(block, g)
-
-        @pl.when(z < n_z - 1)
-        def _():
-            lane_copy(block, g).start()
-
-        cross_copy(block, g).start()
+        send_on(block, g)
+        if g == last:
+
+            @pl.when(is_first)
+            def _():
+                arrived(block + other - ctx, g)
+                send_on(block + other - ctx, g)
+
+            @pl.when(jnp.logical_not(is_first))
+            def _():
+                cross_copy(block, g).start()
+
+        else:
+            cross_copy(block, g).start()
 
     for g in range(local_kv):
         attend(ctx, 1, True, g)
@@ -313,21 +331,39 @@
 
         @pl.when(z > 0)
         def _():
-            pass_on(ctx - 2, g)
+            pass_on(ctx - 2, g, z == 1)
 
         @pl.when(x == 1)
         def _():
             arrived(ctx - 1, g)
+            if g == last:
+
+                @pl.when(z == 0)
+                def _():
+                    send_on(ctx - 1, g)
+
             attend(ctx - 1, 1, False, g)
+
+    @pl.when(jnp.logical_and(x == 0, z == 0))
+    def _():
+        arrived(other, last)
+        send_on(other, last)
 
     def pair_step(step, carry):
         for g in range(local_kv):
 
             @pl.when(step < z)
             def _():
-                pass_on(ctx - 2 * step - 2, g)
-
-            arrived(other - 2 * step, g)
+                pass_on(ctx - 2 * step - 2, g, step + 1 == z)
+
+            if g == last:
+
+                @pl.when(step < z)
+                def _():
+                    arrived(other - 2 * step, g)
+
+            else:
+                arrived(other - 2 * step, g)
             attend(2 * (z - step), 2, False, g)
         return carry
 
@@ -345,7 +381,7 @@
 
     for g in range(local_kv):
 
-        @pl.when(x == 0)
+        @pl.when(crosses_own(g))
         def _():
             cross_copy(ctx, g).wait_send()
 
@@ -356,15 +392,27 @@
     def drain(step, carry):
         block = ctx - 2 * step
         for g in range(local_kv):
-            cross_copy(block, g).wait_send()
 
             @pl.when(z < n_z - 1)
             def _():
                 lane_copy(block, g).wait_send()
 
+            if g == last:
+
+                @pl.when(step < z)
+                def _():
+                    cross_copy(block, g).wait_send()
+
+            else:
+                cross_copy(block, g).wait_send()
+
         return carry
 
     lax.fori_loop(1, z + 1, drain, 0)
+
+    @pl.when(z < n_z - 1)
+    def _():
+        lane_copy(1 - x, last).wait_send()
 
 
 def on_device(

time: 26.1 us -> 25.8 us (0.989)
  Pallas kernels: 24 us -> 23.7 us
    pallas_call x1, Pallas kernels: 24 us -> 23.7 us  [on_device(): pl.pallas_call(functools.partial(kernel, n_ctx, n_head), out_shape=jax.Sh...]
where the time goes in v3:
time: 25.8 us; the launch traced here: 25.6 us
  Pallas kernels  23.7 us (92%)
  local copies, waits for them, and re-layouts  1.88 us (7%)
    pallas_call x1, Pallas kernels, on_device(): pl.pallas_call(functools.partial(kernel, n_ctx, n_head), out_shape=jax.Sh...  23.7 us
    unnamed x1, local copies, waits for them, and re-layouts  1.88 us

profile of v3, /device:TPU:24, one launch (start us, length us, event | category | flops | bytes accessed | tf_op | source)
XLA Modules:
  0.0 25.6 jit_solution(3445590584579880412)
XLA Ops:
  0.0 23.7 %lora_attention.1 = bf16[128,2048]{1,0:T(8,128)(2,1)} custom-call(bf16[128,2048]{1,0:T(8,128)(2,1)} %act_hbm.1, bf16[2048,768]{1,0:T(8,128)(2,1)} %down_hbm.1, s32[2,128]{1,0:T(2,128)} %bitcast.2, f32[2,128]{1,0:T(2,128)} %bitcast.3, bf16[128,2048]{1,0:T(8,128)(2,1)} %qbase_hbm.1, bf16[128,256]{1,0:T(8,128)(2,1)} %kbase_hbm.1, bf16[128,256]{1,0:T(8,128)(2,1)} %vbase_hbm.1, ...), custom_call_target="tpu_custom_call" | custom-call | tf_op jit(solution)/shard_map/lora_attention/pallas_call | solution.py:444
  23.7 1.9 %copy.13 = bf16[128,2048]{1,0:T(8,128)(2,1)} copy(bf16[128,2048]{1,0:T(8,128)(2,1)} %lora_attention.1) | data formatting | bytes 1048576

commit v4 on v3

--- a/solution.py
+++ b/solution.py
@@ -325,13 +325,14 @@
             cross_copy(block, g).start()
 
     for g in range(local_kv):
+
+        @pl.when(z > 0)
+        def _():
+            pass_on(ctx - 2, g, z == 1)
+
         attend(ctx, 1, True, g)
 
     for g in range(local_kv):
-
-        @pl.when(z > 0)
-        def _():
-            pass_on(ctx - 2, g, z == 1)
 
         @pl.when(x == 1)
         def _():

time: 25.8 us -> 26.2 us (1.016)
  Pallas kernels: 23.7 us -> 24.2 us
    pallas_call x1, Pallas kernels: 23.7 us -> 24.2 us  [on_device(): pl.pallas_call(functools.partial(kernel, n_ctx, n_head), out_shape=jax.Sh...]
where the time goes in v4:
time: 26.2 us; the launch traced here: 26 us
  Pallas kernels  24.2 us (92%)
  local copies, waits for them, and re-layouts  1.88 us (7%)
    pallas_call x1, Pallas kernels, on_device(): pl.pallas_call(functools.partial(kernel, n_ctx, n_head), out_shape=jax.Sh...  24.2 us
    unnamed x1, local copies, waits for them, and re-layouts  1.88 us

profile of v4, /device:TPU:24, one launch (start us, length us, event | category | flops | bytes accessed | tf_op | source)
XLA Modules:
  0.0 26.0 jit_solution(14399405082519428455)
XLA Ops:
  0.0 24.2 %lora_attention.1 = bf16[128,2048]{1,0:T(8,128)(2,1)} custom-call(bf16[128,2048]{1,0:T(8,128)(2,1)} %act_hbm.1, bf16[2048,768]{1,0:T(8,128)(2,1)} %down_hbm.1, s32[2,128]{1,0:T(2,128)} %bitcast.2, f32[2,128]{1,0:T(2,128)} %bitcast.3, bf16[128,2048]{1,0:T(8,128)(2,1)} %qbase_hbm.1, bf16[128,256]{1,0:T(8,128)(2,1)} %kbase_hbm.1, bf16[128,256]{1,0:T(8,128)(2,1)} %vbase_hbm.1, ...), custom_call_target="tpu_custom_call" | custom-call | tf_op jit(solution)/shard_map/lora_attention/pallas_call | solution.py:445
  24.2 1.9 %copy.13 = bf16[128,2048]{1,0:T(8,128)(2,1)} copy(bf16[128,2048]{1,0:T(8,128)(2,1)} %lora_attention.1) | data formatting | bytes 1048576

commit v5 on v3

--- a/solution.py
+++ b/solution.py
@@ -262,7 +262,7 @@
             qs[g, h * rows : (h + 1) * rows, :] = rotated(raw)
 
     factor = math.log2(math.e) / math.sqrt(HD)
-    strip = 2 * rows
+    strip = 4 * rows
 
     def attend(block, count, diagonal, g):
         keys = kv[pl.ds(block, count), g, :, :HD].reshape(count * rows, HD)

time: 25.8 us -> 25.6 us (level)
  no operation moved by 1% of the time
where the time goes in v5:
time: 25.6 us; the launch traced here: 25.4 us
  Pallas kernels  23.5 us (92%)
  local copies, waits for them, and re-layouts  1.88 us (7%)
    pallas_call x1, Pallas kernels, on_device(): pl.pallas_call(functools.partial(kernel, n_ctx, n_head), out_shape=jax.Sh...  23.5 us
    unnamed x1, local copies, waits for them, and re-layouts  1.88 us

profile of v5, /device:TPU:24, one launch (start us, length us, event | category | flops | bytes accessed | tf_op | source)
XLA Modules:
  0.0 25.4 jit_solution(602520982338601596)
XLA Ops:
  0.0 23.5 %lora_attention.1 = bf16[128,2048]{1,0:T(8,128)(2,1)} custom-call(bf16[128,2048]{1,0:T(8,128)(2,1)} %act_hbm.1, bf16[2048,768]{1,0:T(8,128)(2,1)} %down_hbm.1, s32[2,128]{1,0:T(2,128)} %bitcast.2, f32[2,128]{1,0:T(2,128)} %bitcast.3, bf16[128,2048]{1,0:T(8,128)(2,1)} %qbase_hbm.1, bf16[128,256]{1,0:T(8,128)(2,1)} %kbase_hbm.1, bf16[128,256]{1,0:T(8,128)(2,1)} %vbase_hbm.1, ...), custom_call_target="tpu_custom_call" | custom-call | tf_op jit(solution)/shard_map/lora_attention/pallas_call | solution.py:444
  23.5 1.9 %copy.13 = bf16[128,2048]{1,0:T(8,128)(2,1)} copy(bf16[128,2048]{1,0:T(8,128)(2,1)} %lora_attention.1) | data formatting | bytes 1048576
